TPU v7x, 128 devices: a whole 4x4x4 slice. The times are simulated.
128 devices in a mesh: rep: 2 (over core), dp: 8 (over y_hi, x), tensor: 8 (over z, y_lo).
Axes of the slice: x: 4, y: 4 (y_hi: 2, y_lo: 2; y = y_hi * 2 + y_lo), z: 4, core: 2. Of those that a mesh axis runs over, the one named last changes fastest.
Arguments:
- frames: bfloat16 [64, 384, 8, 128], P(('rep', 'dp'), 'tensor'), may hold values from -6 to 6
- weight: bfloat16 [384, 3, 3, 3, 384], P('tensor'), may hold values from -0.0625 to 0.0625
- cotangent: bfloat16 [64, 384, 8, 128], P(('rep', 'dp'), 'tensor'), may hold values from -6 to 6
- prev_owner: int32 [16], replicated, may hold values from -1 to 15, as said below
- lengths: int32 [16], replicated, may hold values from 1 to 4, as said below
Outputs:
- output: bfloat16 [64, 384, 8, 128], P(('rep', 'dp'), 'tensor')
- input_grad: float32 [64, 384, 8, 128], P(('rep', 'dp'), 'tensor')
- weight_grad: float32 [384, 3, 3, 3, 384], P('tensor')
Inputs may be any that keep to these rules, and one draw needn't show every extreme that they name: `prev_owner`: each segment index appears at most once; segment 0 of every clip has -1; clips form chains without loops. A segment named in prev_owner has lengths 4; only a clip's last segment may be shorter.
All inputs are finite; a program needn't handle non-finite values.
Results may differ from a plain program's by a relative error of at most 0.0034.
Values may be sent and summed in bfloat16 or wider, within the bound.
No kernel may reach another device: no remote copies, remote signals or barrier semaphores. Data moves between devices by JAX's collectives and lax.ppermute only.
A program may use at most 128 MiB of HBM per device.

v0:
```python
import functools
import math

import jax
import jax.numpy as jnp
from jax import lax
from jax.experimental import pallas as pl
from jax.experimental.pallas import tpu as pltpu
from jax.sharding import PartitionSpec as P

BF16 = jnp.bfloat16
F32 = jnp.float32
MIB = 1024 * 1024
ANY = pl.BlockSpec(memory_space=pl.ANY)
VMEM = pl.BlockSpec(memory_space=pltpu.VMEM)
SMEM = pl.BlockSpec(memory_space=pltpu.SMEM)

PLACES = ((0, 0), (0, 1), (1, 0), (3, 0), (1, 1), (3, 1), (2, 0), (2, 1))


def tensor_index(ring, pair):
    return ring * 2 + pair


class Group:
    def __init__(self, name, index_of, coords):
        self.name = name
        self.index_of = index_of
        me = lax.axis_index(name)
        self.ring, self.pair = coords(me)
        cells = [(r, p) for r in range(4) for p in range(2)]
        self.perm_up = [(index_of(r, p), index_of((r + 1) % 4, p)) for r, p in cells]
        self.perm_down = [(index_of(r, p), index_of((r + 3) % 4, p)) for r, p in cells]
        self.perm_swap = [(index_of(r, p), index_of(r, 1 - p)) for r, p in cells]

    def up(self, x):
        return lax.ppermute(x, self.name, self.perm_up)

    def down(self, x):
        return lax.ppermute(x, self.name, self.perm_down)

    def swap(self, x):
        return lax.ppermute(x, self.name, self.perm_swap)

    def absolute(self):
        return [self.index_of((self.ring + dr) % 4, self.pair ^ dp) for dr, dp in PLACES]

    def gather(self, x):
        half = x.shape[0] // 2
        following, prev, pair = lax.optimization_barrier((self.down(x), self.up(x), self.swap(x)))
        pair_next = self.swap(following)
        pair_prev = self.up(pair)
        second = self.down(following)
        far_a = self.down(pair_next[:half])
        far_b = self.up(pair_prev[half:])
        return [x, pair, following, prev, pair_next, pair_prev, second, far_a, far_b]

    def begin_sum(self, parts):
        far_a, far_b = parts[7:]
        return self.up(far_a), self.down(far_b)

    def end_sum(self, parts, arrived):
        own, pair, following, prev, pair_next, pair_prev, second = parts[:7]
        in_a, in_b = arrived
        got_swap = self.swap(added(pair_next, jnp.concatenate([in_a, jnp.zeros_like(in_a)], 0)))
        got_down = self.down(added(pair_prev, jnp.concatenate([jnp.zeros_like(in_b), in_b], 0)))
        got_up, from_prev = self.up(second), self.down(prev)
        last_up = self.up(added(following, got_swap, got_up))
        last_swap = self.swap(added(pair, got_down))
        return sum(x.astype(F32) for x in (own, from_prev, last_up, last_swap))


def added(*terms):
    return sum(x.astype(F32) for x in terms).astype(BF16)


def shifted(x, by):
    lanes = x.shape[-1]
    column = lax.broadcasted_iota(jnp.int32, x.shape, x.ndim - 1) % 128
    rolled = pltpu.roll(x, by % lanes, x.ndim - 1)
    edge = 0 if by == 1 else 127
    return jnp.where(column == edge, 0.0, rolled)


def fill_taps(live_ref, m_ref, head_ref, taps):
    rows, width, lanes = m_ref.shape
    frames = taps.shape[2] // 128
    taps[0] = jnp.zeros(taps.shape[1:], BF16)
    taps[rows + 1] = jnp.zeros(taps.shape[1:], BF16)
    for h in range(rows):
        whole = jnp.concatenate([m_ref[h], head_ref[h]], 1).astype(F32)
        wide = jnp.concatenate(
            [
                jnp.where(live_ref[f] > 0, whole[:, f * 128 : f * 128 + 128], 0.0)
                for f in range(frames)
            ],
            1,
        )
        taps[h + 1, 0:width] = shifted(wide, -1).astype(BF16)
        taps[h + 1, width : 2 * width] = wide.astype(BF16)
        taps[h + 1, 2 * width : 3 * width] = shifted(wide, 1).astype(BF16)


def input_grad_kernel(place_ref, live_ref, m_ref, head_ref, w_ref, *rest):
    outs, (taps, wt, parts) = rest[:9], rest[9:]
    rows, width, lanes = m_ref.shape
    half = rows // 2
    fill_taps(live_ref, m_ref, head_ref, taps)
    depth = 3 * 3 * width
    for a in range(3):
        block = jnp.concatenate([w_ref[a * 3 + b] for b in range(3)], 0)
        wt[:, a * depth : (a + 1) * depth] = block.T

    for h in range(rows):
        stack = jnp.reshape(taps[h : h + 3], (depth, taps.shape[2]))
        for start in range(0, lanes, 256):
            rhs = jnp.concatenate(
                [stack[:, (2 - a) * 128 + start : (2 - a) * 128 + start + 256] for a in range(3)], 0
            )
            total = jnp.dot(wt[...], rhs, preferred_element_type=F32).astype(BF16)
            for t in range(8):
                parts[t, :, start : start + 256] = total[t * width : (t + 1) * width]
        for r in range(8):
            target = outs[r].at[h] if r < 7 else outs[7 + h // half].at[h % half]
            target[...] = parts[place_ref[r]]


def pick_kernel(row_ref, from_ref, own_ref, other_ref, out_ref):
    for d in range(out_ref.shape[0]):
        own, other = own_ref[row_ref[d]], other_ref[row_ref[d]]
        chosen = jnp.where(from_ref[d] == 1, own, other)
        out_ref[d] = jnp.where(from_ref[d] == 0, jnp.zeros_like(chosen), chosen)


def assemble_kernel(scale, row_ref, from_ref, own_ref, other_ref, out_ref):
    count, summed = own_ref.shape[0], own_ref.shape[1] - other_ref.shape[1]
    total = own_ref[0, :summed].astype(F32)
    for d in range(1, count):
        total = total + own_ref[d, :summed].astype(F32)
    share = (total * scale).astype(BF16)
    for d in range(count):
        out_ref[d, :summed] = share
        own, other = own_ref[row_ref[d], summed:], other_ref[row_ref[d]]
        chosen = jnp.where(from_ref[d] == 1, own, other)
        out_ref[d, summed:] = jnp.where(from_ref[d] == 0, jnp.zeros_like(chosen), chosen)


CHUNK = 2


def start_loads(place_ref, blocks, x, sems):
    rows, width = blocks[0].shape[0], blocks[0].shape[1]
    half = rows // 2
    x[0] = jnp.zeros(x.shape[1:], BF16)
    x[rows + 1] = jnp.zeros(x.shape[1:], BF16)
    lists = []
    for part in range(rows // CHUNK):
        first = part * CHUNK
        copies = []
        for r in range(8):
            channel = pl.ds(pl.multiple_of(place_ref[r] * width, 16), width)
            block, skip = (blocks[r], 0) if r < 7 else (blocks[7 + first // half], first // half * half)
            copies.append(
                pltpu.make_async_copy(
                    block.at[first - skip : first - skip + CHUNK],
                    x.at[first + 1 : first + 1 + CHUNK, channel],
                    sems.at[part, r],
                )
            )
            copies[-1].start()
        lists.append(copies)
    return lists


def wait_for(copies):
    for copy in copies:
        copy.wait()


def forward_kernel(place_ref, after_ref, *rest):
    del after_ref
    blocks, (w_ref, out_ref, carry_ref, x, sems) = rest[:9], rest[9:]
    rows, width, lanes = out_ref.shape
    loads = start_loads(place_ref, blocks, x, sems)
    lhs = jnp.concatenate(
        [jnp.concatenate([w_ref[a * 3 + 2 - b] for a in range(3)], 0) for b in range(3)], 1
    )
    wait_for(loads[0])
    for h in range(rows):
        if (h + 1) % CHUNK == 0 and h + 1 < rows:
            wait_for(loads[(h + 1) // CHUNK])
        stack = jnp.reshape(x[h : h + 3], (3 * x.shape[1], lanes))
        y = jnp.dot(lhs, stack, preferred_element_type=F32)
        sums = []
        for e in range(3):
            frames = []
            for g in range(lanes // 128 + 2):
                terms = []
                for a in range(3):
                    f = g + a - 2
                    if 0 <= f < lanes // 128:
                        row = (a * 3 + e) * width
                        terms.append(y[row : row + width, f * 128 : f * 128 + 128])
                total = terms[0]
                for term in terms[1:]:
                    total = total + term
                frames.append(total)
            sums.append(jnp.concatenate(frames, 1))
        result = sums[1] + shifted(sums[0], 1) + shifted(sums[2], -1)
        out_ref[h] = result[:, :lanes]
        carry_ref[h, :width] = result[:, lanes : lanes + 128].astype(BF16)
        carry_ref[h, width:] = result[:, lanes + 128 :].astype(BF16)


def kernel_grad_kernel(place_ref, live_ref, rep_ref, after_ref, *rest):
    del after_ref
    blocks, (m_ref, head_ref, mine_ref, theirs_ref, x, taps, total, result, sems, out_sems) = rest[:9], rest[9:]
    rows, width, lanes = m_ref.shape
    loads = start_loads(place_ref, blocks, x, sems)
    fill_taps(live_ref, m_ref, head_ref, taps)
    depth = 9 * width
    result[9 * depth :, :] = jnp.zeros((result.shape[0] - 9 * depth, 128), F32)
    for h in range(rows):
        if h % CHUNK == 0:
            wait_for(loads[h // CHUNK])
        stack = jnp.reshape(taps[h : h + 3], (depth, taps.shape[2]))
        right = x[h + 1]
        for a in range(3):
            left = stack[:, (2 - a) * 128 : (2 - a) * 128 + lanes]
            product = lax.dot_general(
                left, right, (((1,), (1,)), ((), ())), preferred_element_type=F32
            )
            if h == 0:
                total[a] = product
            elif h < rows - 1:
                total[a] += product
            else:
                product = total[a] + product
                for block in range(3):
                    row = (a * 3 + block) * depth
                    result[row : row + depth, :] = product[:, block * 128 : block * 128 + 128]
    half = result.shape[0] // 2
    copies = []
    for slot, (target, rep) in enumerate(((theirs_ref, 1 - rep_ref[0]), (mine_ref, rep_ref[0]))):
        source = result.at[pl.ds(pl.multiple_of(rep * half, 16), half)]
        copies.append(pltpu.make_async_copy(source, target, out_sems.at[slot]))
        copies[-1].start()
    wait_for(copies)


def params(mib):
    return pltpu.CompilerParams(vmem_limit_bytes=mib * MIB)


def cost(flops, size):
    return pl.CostEstimate(flops=flops, bytes_accessed=size, transcendentals=0)


FLOPS = 2 * 27 * 48 * 384 * 4096


def input_partials(place, live, m, head, weight):
    rows, width, lanes = m.shape
    channels = weight.shape[2]
    whole = jax.ShapeDtypeStruct((rows, width, lanes), BF16)
    half = jax.ShapeDtypeStruct((rows // 2, width, lanes), BF16)
    return pl.pallas_call(
        input_grad_kernel,
        out_shape=[whole] * 7 + [half] * 2,
        in_specs=[SMEM, SMEM, VMEM, VMEM, VMEM],
        out_specs=[VMEM] * 9,
        scratch_shapes=[
            pltpu.VMEM((rows + 2, 3 * width, lanes + 256), BF16),
            pltpu.VMEM((channels, 27 * width), BF16),
            pltpu.VMEM((8, width, lanes), BF16),
        ],
        compiler_params=params(20),
        cost_estimate=cost(FLOPS, 5_000_000),
        name="input_partials",
    )(place, live, m, head, weight)


def pick(row, origin, own, other):
    return pl.pallas_call(
        pick_kernel,
        out_shape=jax.ShapeDtypeStruct(own.shape, own.dtype),
        in_specs=[SMEM, SMEM, VMEM, VMEM],
        out_specs=VMEM,
        compiler_params=params(4),
        name="pick",
    )(row, origin, own, other)


def assemble(scale, row, origin, own, other):
    return pl.pallas_call(
        functools.partial(assemble_kernel, scale),
        out_shape=jax.ShapeDtypeStruct(own.shape, own.dtype),
        in_specs=[SMEM, SMEM, VMEM, VMEM],
        out_specs=VMEM,
        compiler_params=params(6),
        name="assemble",
    )(row, origin, own, other)


def forward(place, after, blocks, weight):
    rows, width, lanes = blocks[0].shape
    channels = weight.shape[2]
    return pl.pallas_call(
        forward_kernel,
        out_shape=[
            jax.ShapeDtypeStruct((rows, width, lanes), F32),
            jax.ShapeDtypeStruct((rows, 2 * width, 128), BF16),
        ],
        in_specs=[SMEM] + [ANY] * 10 + [VMEM],
        out_specs=[VMEM, VMEM],
        scratch_shapes=[
            pltpu.VMEM((rows + 2, channels, lanes), BF16),
            pltpu.SemaphoreType.DMA((rows // CHUNK, 8)),
        ],
        compiler_params=params(20),
        cost_estimate=cost(FLOPS, 5_000_000),
        name="forward",
    )(place, after, *blocks, weight)


def kernel_grad(place, live, rep, after, blocks, m, head):
    rows, width, lanes = m.shape
    channels = 8 * width
    return pl.pallas_call(
        kernel_grad_kernel,
        out_shape=[jax.ShapeDtypeStruct((2048, 128), F32)] * 2,
        in_specs=[SMEM] * 3 + [ANY] * 10 + [VMEM, VMEM],
        out_specs=[ANY, ANY],
        scratch_shapes=[
            pltpu.VMEM((rows + 2, channels, lanes), BF16),
            pltpu.VMEM((rows + 2, 3 * width, lanes + 256), BF16),
            pltpu.VMEM((3, 9 * width, channels), F32),
            pltpu.VMEM((4096, 128), F32),
            pltpu.SemaphoreType.DMA((rows // CHUNK, 8)),
            pltpu.SemaphoreType.DMA((2,)),
        ],
        compiler_params=params(20),
        cost_estimate=cost(FLOPS, 6_000_000),
        name="kernel_grad",
    )(place, live, rep, after, *blocks, m, head)


def to_rows(x):
    f, c, h, w = x.shape
    return x.transpose(2, 1, 0, 3).reshape(h, c, f * w)


def from_rows(x):
    h, c, lanes = x.shape
    return x.reshape(h, c, lanes // 128, 128).transpose(2, 1, 0, 3)


def core_swap(x):
    return lax.ppermute(x, "rep", [(0, 1), (1, 0)])


def exchange(x):
    return lax.all_to_all(x, "dp", 0, 0, tiled=True)


def asked_for(source):
    rep = lax.axis_index("rep")
    wanted = lax.dynamic_slice_in_dim(source, rep * 8, 8, 0)
    row = jnp.maximum(wanted, 0) % 8
    origin = jnp.where(wanted < 0, 0, jnp.where(wanted // 8 == rep, 1, 2)).astype(jnp.int32)
    return row, origin


def handed_on(own, source):
    row, origin = asked_for(source)
    return pick(row, origin, own, core_swap(own))


def first_exchange(mine, theirs, payload):
    pair = (mine + core_swap(theirs)).astype(BF16).reshape(8, 256, 128)
    return jnp.concatenate([pair, payload], 1)


def both_cores(spread):
    rep = lax.axis_index("rep")
    there = core_swap(spread)
    half, there = (x[:, :256].reshape(2048, 128) for x in (spread, there))
    low = jnp.where(rep == 0, half, there)
    high = jnp.where(rep == 0, there, half)
    return jnp.concatenate([low, high], 0)


def per_device(frames, weight, cotangent, prev_owner, lengths):
    seg_len, width, height, columns = frames.shape
    channels = weight.shape[4]
    rep, me = lax.axis_index("rep"), lax.axis_index("dp")
    member = rep * 8 + me
    tensor = Group("tensor", tensor_index, lambda i: (i // 2, i % 2))
    place = jnp.stack(tensor.absolute()).astype(jnp.int32)
    segments = jnp.arange(prev_owner.shape[0], dtype=jnp.int32)
    follows = prev_owner[None, :] == segments[:, None]
    follower = jnp.max(jnp.where(follows, segments[None, :], -1), 1)

    x = to_rows(frames)
    m = to_rows(cotangent)
    rows = weight.transpose(1, 2, 3, 0, 4)[:, ::-1].reshape(9, 3 * width, channels)

    payload, x = lax.optimization_barrier((m[:, :, :256], x))
    payload = exchange(payload)
    blocks = tensor.gather(x)
    payload, _ = lax.optimization_barrier((payload, (blocks[1], blocks[2])))
    head = exchange(handed_on(payload, follower))
    keep = jnp.arange(seg_len) < lengths[member]
    keep_head = jnp.arange(2) < lengths[jnp.maximum(follower[member], 0)]
    live = jnp.concatenate([keep, keep_head]).astype(jnp.int32)

    partials = input_partials(place, live, m, head, rows)
    partials, blocks = lax.optimization_barrier((partials, blocks))
    arrived = tensor.begin_sum(partials)
    mine, theirs = kernel_grad(place, live, rep.astype(jnp.int32)[None], partials[0], blocks, m, head)
    conv, carry = forward(place, theirs, blocks, rows)
    spread = first_exchange(mine, theirs, carry)
    arrived, spread = lax.optimization_barrier((arrived, spread))
    input_grad = from_rows(tensor.end_sum(partials, arrived))
    conv = conv.reshape(height, width, seg_len, columns).transpose(2, 1, 0, 3)
    spread = exchange(spread)

    cells = prev_owner.shape[0] * seg_len * height * columns
    row, origin = asked_for(prev_owner)
    spread = exchange(
        assemble(1.0 / math.sqrt(cells), row, origin, spread, core_swap(spread[:, 256:]))
    )
    received = spread[:, 256:]
    total = both_cores(spread)
    total = total[: 81 * width].reshape(3, 3, 3, 3, width, 128)
    weight_grad = total[:, :, ::-1].transpose(4, 0, 2, 3, 1, 5).reshape(weight.shape).astype(F32)

    received = received.reshape(height, 2, width, columns).transpose(1, 2, 0, 3).astype(F32)
    conv = conv + jnp.concatenate([received, jnp.zeros_like(received)], 0)
    output = jnp.where(keep[:, None, None, None], conv, 0.0).astype(BF16)
    return (output, input_grad, weight_grad)


def solution(mesh):
    split = P(("rep", "dp"), "tensor", None, None)
    kernel = P("tensor", None, None, None, None)
    return jax.shard_map(
        per_device,
        mesh=mesh,
        in_specs=(split, kernel, split, P(), P()),
        out_specs=(split, split, kernel),
        check_vma=False,
    )
```

profile of v0, /device:TPU:1, one launch (start us, length us, event | category | flops | bytes accessed | tf_op | source)
XLA Modules:
  0.0 128.2 jit_solution(16415502467195335146)
XLA Ops:
  0.7 1.3 %copy.25 = bf16[8,48,4,128]{3,2,1,0:T(4,128)(2,1)S(1)} copy(bf16[8,48,4,128]{3,0,1,2:T(8,128)(2,1)} %bitcast.49) | data formatting | bytes 786432 | tf_op jit(solution)/shard_map/transpose | solution.py:350
  3.3 4.7 %collective-permute-start = (bf16[8,48,512]{2,1,0:T(8,128)(2,1)S(1)}, bf16[8,48,512]{2,1,0:T(8,128)(2,1)}, u32[]{:S(2)}, u32[]{:S(2)}) collective-permute-start(bf16[8,48,512]{2,1,0:T(8,128)(2,1)S(1)} %reshape.47.rest_0_), channel_id=1, source_target_pairs={{0,6},{1,7},{2,0},{3,1},{4,2},{5,3},{6,4},{7,5},{8,14},{9,15},{10,... | collective-permute-start | bytes 1179656 | tf_op jit(solution)/shard_map/ppermute | solution.py:40
  8.0 1.3 %collective-permute-start.2 = (bf16[8,48,512]{2,1,0:T(8,128)(2,1)S(1)}, bf16[8,48,512]{2,1,0:T(8,128)(2,1)S(1)}, u32[]{:S(2)}, u32[]{:S(2)}) collective-permute-start(bf16[8,48,512]{2,1,0:T(8,128)(2,1)S(1)} %reshape.47.rest_0_), channel_id=1, source_target_pairs={{0,1},{1,0},{2,3},{3,2},{4,5},{5,4},{6,7},{7,6},{8,9},{9,8},{10,11... | collective-permute-start | bytes 1179656 | tf_op jit(solution)/shard_map/ppermute | solution.py:43
  9.3 6.4 %all-to-all-start = ((bf16[8,48,256]{2,1,0:T(8,128)(2,1)}), bf16[8,48,256]{2,1,0:T(8,128)(2,1)S(1)}, u32[]{:S(2)}, u32[]{:S(2)}) async-start(bf16[8,48,256]{2,1,0:T(8,128)(2,1)} %slice.32), calls=%async_computation | async-start | bytes 393216 | tf_op jit(solution)/shard_map/all_to_all | solution.py:363
  19.6 1.3 %collective-permute-start.4 = (bf16[8,48,512]{2,1,0:T(8,128)(2,1)}, bf16[8,48,512]{2,1,0:T(8,128)(2,1)S(1)}, u32[]{:S(2)}, u32[]{:S(2)}) collective-permute-start(bf16[8,48,512]{2,1,0:T(8,128)(2,1)} %collective-permute-done.rest_2_), channel_id=1, source_target_pairs={{0,1},{1,0},{2,3},{3,2},{4,5},{5,4},{6,7},{7,6},{8,9},{9,8},{10,11... | collective-permute-start | bytes 1179656 | tf_op jit(solution)/shard_map/ppermute | solution.py:43
  20.9 2.0 %all-to-all-done.own_ref = bf16[8,48,256]{2,1,0:T(8,128)(2,1)S(1)} async-done(((bf16[8,48,256]{2,1,0:T(8,128)(2,1)}), bf16[8,48,256]{2,1,0:T(8,128)(2,1)S(1)}, u32[]{:S(2)}, u32[]{:S(2)}) %all-to-all-start) | async-done | bytes 196640 | tf_op jit(solution)/shard_map/all_to_all | solution.py:363
  23.0 2.7 %collective-permute-start.3 = (bf16[8,48,256]{2,1,0:T(8,128)(2,1)S(1)}, bf16[8,48,256]{2,1,0:T(8,128)(2,1)S(1)}, u32[]{:S(2)}, u32[]{:S(2)}) collective-permute-start(bf16[8,48,256]{2,1,0:T(8,128)(2,1)S(1)} %all-to-all-done.own_ref), channel_id=1, source_target_pairs={{0,64},{64,0},{1,65},{65,1},{2,66},{66,2},{3,67},{67,3},{4,68},{68... | collective-permute-start | bytes 589832 | tf_op jit(solution)/shard_map/ppermute | solution.py:359
  27.9 3.8 %all-to-all-start.1 = ((bf16[8,48,256]{2,1,0:T(8,128)(2,1)}), bf16[8,48,256]{2,1,0:T(8,128)(2,1)S(1)}, u32[]{:S(2)}, u32[]{:S(2)}) async-start(bf16[8,48,256]{2,1,0:T(8,128)(2,1)} %pick.1), calls=%async_computation.1 | async-start | bytes 393216 | tf_op jit(solution)/shard_map/all_to_all | solution.py:363
  32.4 3.0 %collective-permute-start.6 = (bf16[8,48,512]{2,1,0:T(8,128)(2,1)}, bf16[8,48,512]{2,1,0:T(8,128)(2,1)}, u32[]{:S(2)}, u32[]{:S(2)}) collective-permute-start(bf16[8,48,512]{2,1,0:T(8,128)(2,1)} %collective-permute-done.rest_2_), channel_id=1, source_target_pairs={{0,6},{1,7},{2,0},{3,1},{4,2},{5,3},{6,4},{7,5},{8,14},{9,15},{10,... | collective-permute-start | bytes 1179656 | tf_op jit(solution)/shard_map/ppermute | solution.py:40
  36.0 1.3 %rev.6 = bf16[3,3,3,48,384]{4,3,2,1,0:T(8,128)(2,1)S(1)} reverse(bf16[3,3,3,48,384]{4,3,2,1,0:T(8,128)(2,1)} %bitcast.45), dimensions={1} | reverse | bytes 1990656 | tf_op jit(solution)/shard_map/rev | solution.py:406
  38.2 1.3 %collective-permute-start.7 = (bf16[4,48,512]{2,1,0:T(8,128)(2,1)}, bf16[4,48,512]{2,1,0:T(8,128)(2,1)}, u32[]{:S(2)}, u32[]{:S(2)}) collective-permute-start(bf16[4,48,512]{2,1,0:T(8,128)(2,1)} %slice.33), channel_id=1, source_target_pairs={{0,6},{1,7},{2,0},{3,1},{4,2},{5,3},{6,4},{7,5},{8,14},{9,15},{10,... | collective-permute-start | bytes 589832 | tf_op jit(solution)/shard_map/ppermute | solution.py:40
  41.1 6.1 %input_partials.1 = (bf16[8,48,512]{2,1,0:T(8,128)(2,1)S(1)}, bf16[8,48,512]{2,1,0:T(8,128)(2,1)S(1)}, bf16[8,48,512]{2,1,0:T(8,128)(2,1)S(1)}, bf16[8,48,512]{2...) custom-call(s32[8]{0:T(128)S(1)} %stack.35.place_ref, ...), custom_call_target="tpu_custom_call" | custom-call | flops 4076863488 | bytes 5000000 | tf_op jit(solution)/shard_map/input_partials/pallas_call | solution.py:267
  48.0 9.1 %kernel_grad.1 = (f32[2048,128]{1,0:T(8,128)S(1)}, f32[2048,128]{1,0:T(8,128)S(1)}) custom-call(s32[8]{0:T(128)S(1)} %stack.35.place_ref, s32[6]{0:T(128)S(1)} %copy-done.14, s32[1]{0:T(128)} %bitcast.11.rep_ref, bf16[8,48,512]{2,1,0:T(8,128)(2,1)S(1)} %get-tuple-element.58.after_ref, bf16[8,48,512]{2,1,0:T(8,128)(2,1)S(1)} %reshape.47.rest_0_, ...), custom_call_target="tpu_custom_call" | custom-call | flops 4076863488 | bytes 6000000 | tf_op jit(solution)/shard_map/kernel_grad/pallas_call | solution.py:329
  57.1 1.6 %collective-permute-start.11 = (f32[2048,128]{1,0:T(8,128)S(1)}, f32[2048,128]{1,0:T(8,128)S(1)}, u32[]{:S(2)}, u32[]{:S(2)}) collective-permute-start(f32[2048,128]{1,0:T(8,128)S(1)} %get-tuple-element.68.after_ref), channel_id=1, source_target_pairs={{0,64},{64,0},{1,65},{65,1},{2,66},{66,2},{3,67},{67,3},{4,68},{68... | collective-permute-start | bytes 3145736 | tf_op jit(solution)/shard_map/ppermute | solution.py:359
  59.9 2.0 %collective-permute-start.10 = (bf16[4,48,512]{2,1,0:T(8,128)(2,1)S(1)}, bf16[4,48,512]{2,1,0:T(8,128)(2,1)}, u32[]{:S(2)}, u32[]{:S(2)}) collective-permute-start(bf16[4,48,512]{2,1,0:T(8,128)(2,1)S(1)} %get-tuple-element.71), channel_id=1, source_target_pairs={{0,6},{1,7},{2,0},{3,1},{4,2},{5,3},{6,4},{7,5},{8,14},{9,15},{10,... | collective-permute-start | bytes 589832 | tf_op jit(solution)/shard_map/ppermute | solution.py:40
  61.9 7.9 %forward.1 = (f32[8,48,512]{2,1,0:T(8,128)S(1)}, bf16[8,96,128]{2,1,0:T(8,128)(2,1)S(1)}) custom-call(s32[8]{0:T(128)S(1)} %stack.35.place_ref, f32[2048,128]{1,0:T(8,128)S(1)} %get-tuple-element.68.after_ref, bf16[8,48,512]{2,1,0:T(8,128)(2,1)S(1)} %reshape.47.rest_0_, bf16[8,48,512]{2,1,0:T(8,128)(2,1)S(1)} %copy-done.10, ...), custom_call_target="tpu_custom_call" | custom-call | flops 4076863488 | bytes 5000000 | tf_op jit(solution)/shard_map/forward/pallas_call | solution.py:308
  70.9 6.7 %all-to-all-start.2 = ((bf16[8,352,128]{2,1,0:T(8,128)(2,1)}), bf16[8,352,128]{2,1,0:T(8,128)(2,1)S(1)}, u32[]{:S(2)}, u32[]{:S(2)}) async-start(bf16[8,352,128]{2,1,0:T(8,128)(2,1)} %pad_maximum_fusion.1), calls=%async_computation.2 | async-start | bytes 1441792 | tf_op jit(solution)/shard_map/all_to_all | solution.py:363
  77.6 1.8 %add_convert_fusion.2 = bf16[8,48,512]{2,1,0:T(8,128)(2,1)} fusion(bf16[8,48,512]{2,1,0:T(8,128)(2,1)} %copy-done.2, bf16[4,48,512]{2,1,0:T(8,128)(2,1)} %collective-permute-done.10), kind=kLoop, calls=%fused_computation.10 | loop fusion | flops 786432 | bytes 983040 | tf_op jit(solution)/shard_map/convert_element_type | solution.py:74
  79.4 1.5 %collective-permute-start.17 = (bf16[8,48,512]{2,1,0:T(8,128)(2,1)}, bf16[8,48,512]{2,1,0:T(8,128)(2,1)}, u32[]{:S(2)}, u32[]{:S(2)}) collective-permute-start(bf16[8,48,512]{2,1,0:T(8,128)(2,1)} %add_convert_fusion.2), channel_id=1, source_target_pairs={{0,6},{1,7},{2,0},{3,1},{4,2},{5,3},{6,4},{7,5},{8,14},{9,15},{10,... | collective-permute-start | bytes 1179656 | tf_op jit(solution)/shard_map/ppermute | solution.py:40
  80.9 10.5 %all-to-all-done.2.own_ref = bf16[8,352,128]{2,1,0:T(8,128)(2,1)S(1)} async-done(((bf16[8,352,128]{2,1,0:T(8,128)(2,1)}), bf16[8,352,128]{2,1,0:T(8,128)(2,1)S(1)}, u32[]{:S(2)}, u32[]{:S(2)}) %all-to-all-start.2) | async-done | bytes 720928 | tf_op jit(solution)/shard_map/all_to_all | solution.py:363
  93.2 1.5 %collective-permute-start.13 = (bf16[8,48,512]{2,1,0:T(8,128)(2,1)}, bf16[8,48,512]{2,1,0:T(8,128)(2,1)S(1)}, u32[]{:S(2)}, u32[]{:S(2)}) collective-permute-start(bf16[8,48,512]{2,1,0:T(8,128)(2,1)} %copy-done.11), channel_id=1, source_target_pairs={{0,6},{1,7},{2,0},{3,1},{4,2},{5,3},{6,4},{7,5},{8,14},{9,15},{10,... | collective-permute-start | bytes 1179656 | tf_op jit(solution)/shard_map/ppermute | solution.py:40
  94.7 1.5 %assemble.1 = bf16[8,352,128]{2,1,0:T(8,128)(2,1)} custom-call(s32[8]{0:T(128)S(1)} %get-tuple-element.86.row_ref, s32[8]{0:T(128)S(1)} %get-tuple-element.85.from_ref, bf16[8,352,128]{2,1,0:T(8,128)(2,1)S(1)} %all-to-all-done.2.own_ref, bf16[8,96,128]{2,1,0:T(8,128)(2,1)S(1)} %collective-permute-done.12.other_ref), custom_call_target="tpu_custom_call" | custom-call | tf_op jit(solution)/shard_map/assemble/pallas_call | solution.py:295
  96.3 4.2 %all-to-all-start.3 = ((bf16[8,352,128]{2,1,0:T(8,128)(2,1)}), bf16[8,352,128]{2,1,0:T(8,128)(2,1)}, u32[]{:S(2)}, u32[]{:S(2)}) async-start(bf16[8,352,128]{2,1,0:T(8,128)(2,1)} %assemble.1), calls=%async_computation.3 | async-start | bytes 1441792 | tf_op jit(solution)/shard_map/all_to_all | solution.py:363
  100.5 1.8 %add_convert_fusion.1 = bf16[8,48,512]{2,1,0:T(8,128)(2,1)} fusion(bf16[8,48,512]{2,1,0:T(8,128)(2,1)} %collective-permute-done.17, bf16[8,48,512]{2,1,0:T(8,128)(2,1)S(1)} %get-tuple-element.80), kind=kLoop, calls=%fused_computation.9 | loop fusion | flops 786432 | bytes 1179648 | tf_op jit(solution)/shard_map/convert_element_type | solution.py:74
  102.3 1.5 %collective-permute-start.18 = (bf16[8,48,512]{2,1,0:T(8,128)(2,1)}, bf16[8,48,512]{2,1,0:T(8,128)(2,1)S(1)}, u32[]{:S(2)}, u32[]{:S(2)}) collective-permute-start(bf16[8,48,512]{2,1,0:T(8,128)(2,1)} %add_convert_fusion.1), channel_id=1, source_target_pairs={{0,1},{1,0},{2,3},{3,2},{4,5},{5,4},{6,7},{7,6},{8,9},{9,8},{10,11... | collective-permute-start | bytes 1179656 | tf_op jit(solution)/shard_map/ppermute | solution.py:43
  104.2 2.0 %add_convert_fusion.3 = bf16[8,48,512]{2,1,0:T(8,128)(2,1)} fusion(bf16[8,48,512]{2,1,0:T(8,128)(2,1)} %collective-permute-done.15, bf16[8,48,512]{2,1,0:T(8,128)(2,1)} %collective-permute-done.14, bf16[8,48,512]{2,1,0:T(8,128)(2,1)S(1)} %get-tuple-element.76), kind=kLoop, calls=%fused_computation.11 | loop fusion | flops 1179648 | bytes 1572864 | tf_op jit(solution)/shard_map/convert_element_type | solution.py:74
  106.2 8.2 %all-to-all-done.3 = bf16[8,352,128]{2,1,0:T(8,128)(2,1)} async-done(((bf16[8,352,128]{2,1,0:T(8,128)(2,1)}), bf16[8,352,128]{2,1,0:T(8,128)(2,1)}, u32[]{:S(2)}, u32[]{:S(2)}) %all-to-all-start.3) | async-done | bytes 720928 | tf_op jit(solution)/shard_map/all_to_all | solution.py:363
  115.5 4.7 %collective-permute-done.18 = bf16[8,48,512]{2,1,0:T(8,128)(2,1)S(1)} collective-permute-done((bf16[8,48,512]{2,1,0:T(8,128)(2,1)}, bf16[8,48,512]{2,1,0:T(8,128)(2,1)S(1)}, u32[]{:S(2)}, u32[]{:S(2)}) %collective-permute-start.18) | collective-permute-done | bytes 393248 | tf_op jit(solution)/shard_map/ppermute | solution.py:43
  120.2 1.3 %convert_add_fusion = f32[8,48,512]{2,1,0:T(8,128)S(1)} fusion(bf16[8,48,512]{2,1,0:T(8,128)(2,1)S(1)} %collective-permute-done.18, bf16[8,48,512]{2,1,0:T(8,128)(2,1)} %collective-permute-done.16, bf16[8,48,512]{2,1,0:T(8,128)(2,1)} %copy-done.15, bf16[8,48,512]{2,1,0:T(8,128)(2,1)S(1)} %get-tuple-element.58.after_ref), kind=kLoop, calls=%fused_computation.8 | loop fusion | flops 1376256 | bytes 2359296 | tf_op jit(solution)/shard_map/add | solution.py:70
  121.8 1.3 %copy.36 = f32[8,48,4,128]{3,0,1,2:T(8,128)} copy(f32[8,48,4,128]{3,2,1,0:T(4,128)S(1)} %reshape.51) | data formatting | bytes 1572864 | tf_op jit(solution)/shard_map/reshape | solution.py:355
  125.4 1.3 broadcast_select_fusion.1
  126.8 1.4 %copy_bitcast_fusion = f32[48,3,3,3,384]{4,0,3,2,1:T(8,128)} fusion(bf16[3,3,3,3,48,128]{5,4,3,2,1,0:T(8,128)(2,1)S(1)} %bitcast.41), kind=kLoop, calls=%fused_computation | loop fusion | flops 497664 | bytes 2985984 | tf_op jit(solution)/shard_map/convert_element_type | solution.py:436
  (99 shorter events, 19.5 us)
Async XLA Ops:
  0.6 15.0 %copy-start.20 = (s32[16]{0:T(128)S(1)}, s32[16]{0:T(128)}, u32[]{:S(2)}) copy-start(s32[16]{0:T(128)} %param.8) | copy-start | bytes 196
  0.7 16.4 %copy-start.17 = (s32[16]{0:T(128)S(1)}, s32[16]{0:T(128)}, u32[]{:S(2)}) copy-start(s32[16]{0:T(128)} %param.9) | copy-start | bytes 196
  3.3 14.3 %collective-permute-start = (bf16[8,48,512]{2,1,0:T(8,128)(2,1)S(1)}, bf16[8,48,512]{2,1,0:T(8,128)(2,1)}, u32[]{:S(2)}, u32[]{:S(2)}) collective-permute-start(bf16[8,48,512]{2,1,0:T(8,128)(2,1)S(1)} %reshape.47.rest_0_), channel_id=1, source_target_pairs={{0,6},{1,7},{2,0},{3,1},{4,2},{5,3},{6,4},{7,5},{8,14},{9,15},{10,... | collective-permute-start | bytes 1179656 | tf_op jit(solution)/shard_map/ppermute | solution.py:40
  8.0 10.9 %collective-permute-start.1 = (bf16[8,48,512]{2,1,0:T(8,128)(2,1)S(1)}, bf16[8,48,512]{2,1,0:T(8,128)(2,1)S(1)}, u32[]{:S(2)}, u32[]{:S(2)}) collective-permute-start(bf16[8,48,512]{2,1,0:T(8,128)(2,1)S(1)} %reshape.47.rest_0_), channel_id=1, source_target_pairs={{0,2},{1,3},{2,4},{3,5},{4,6},{5,7},{6,0},{7,1},{8,10},{9,11},{10,... | collective-permute-start | bytes 1179656 | tf_op jit(solution)/shard_map/ppermute | solution.py:37
  8.0 11.6 %collective-permute-start.2 = (bf16[8,48,512]{2,1,0:T(8,128)(2,1)S(1)}, bf16[8,48,512]{2,1,0:T(8,128)(2,1)S(1)}, u32[]{:S(2)}, u32[]{:S(2)}) collective-permute-start(bf16[8,48,512]{2,1,0:T(8,128)(2,1)S(1)} %reshape.47.rest_0_), channel_id=1, source_target_pairs={{0,1},{1,0},{2,3},{3,2},{4,5},{5,4},{6,7},{7,6},{8,9},{9,8},{10,11... | collective-permute-start | bytes 1179656 | tf_op jit(solution)/shard_map/ppermute | solution.py:43
  9.3 13.7 %all-to-all-start = ((bf16[8,48,256]{2,1,0:T(8,128)(2,1)}), bf16[8,48,256]{2,1,0:T(8,128)(2,1)S(1)}, u32[]{:S(2)}, u32[]{:S(2)}) async-start(bf16[8,48,256]{2,1,0:T(8,128)(2,1)} %slice.32), calls=%async_computation | async-start | bytes 393216 | tf_op jit(solution)/shard_map/all_to_all | solution.py:363
  19.6 20.8 %copy-start.9 = (bf16[8,48,512]{2,1,0:T(8,128)(2,1)}, bf16[8,48,512]{2,1,0:T(8,128)(2,1)S(1)}, u32[]{:S(2)}) copy-start(bf16[8,48,512]{2,1,0:T(8,128)(2,1)S(1)} %collective-permute-done.2.rest_1_) | copy-start | bytes 1179652
  19.6 17.8 %collective-permute-start.4 = (bf16[8,48,512]{2,1,0:T(8,128)(2,1)}, bf16[8,48,512]{2,1,0:T(8,128)(2,1)S(1)}, u32[]{:S(2)}, u32[]{:S(2)}) collective-permute-start(bf16[8,48,512]{2,1,0:T(8,128)(2,1)} %collective-permute-done.rest_2_), channel_id=1, source_target_pairs={{0,1},{1,0},{2,3},{3,2},{4,5},{5,4},{6,7},{7,6},{8,9},{9,8},{10,11... | collective-permute-start | bytes 1179656 | tf_op jit(solution)/shard_map/ppermute | solution.py:43
  20.9 18.6 %collective-permute-start.5 = (bf16[8,48,512]{2,1,0:T(8,128)(2,1)S(1)}, bf16[8,48,512]{2,1,0:T(8,128)(2,1)S(1)}, u32[]{:S(2)}, u32[]{:S(2)}) collective-permute-start(bf16[8,48,512]{2,1,0:T(8,128)(2,1)S(1)} %collective-permute-done.2.rest_1_), channel_id=1, source_target_pairs={{0,2},{1,3},{2,4},{3,5},{4,6},{5,7},{6,0},{7,1},{8,10},{9,11},{10,... | collective-permute-start | bytes 1179656 | tf_op jit(solution)/shard_map/ppermute | solution.py:37
  23.0 3.7 %collective-permute-start.3 = (bf16[8,48,256]{2,1,0:T(8,128)(2,1)S(1)}, bf16[8,48,256]{2,1,0:T(8,128)(2,1)S(1)}, u32[]{:S(2)}, u32[]{:S(2)}) collective-permute-start(bf16[8,48,256]{2,1,0:T(8,128)(2,1)S(1)} %all-to-all-done.own_ref), channel_id=1, source_target_pairs={{0,64},{64,0},{1,65},{65,1},{2,66},{66,2},{3,67},{67,3},{4,68},{68... | collective-permute-start | bytes 589832 | tf_op jit(solution)/shard_map/ppermute | solution.py:359
  27.9 12.5 %all-to-all-start.1 = ((bf16[8,48,256]{2,1,0:T(8,128)(2,1)}), bf16[8,48,256]{2,1,0:T(8,128)(2,1)S(1)}, u32[]{:S(2)}, u32[]{:S(2)}) async-start(bf16[8,48,256]{2,1,0:T(8,128)(2,1)} %pick.1), calls=%async_computation.1 | async-start | bytes 393216 | tf_op jit(solution)/shard_map/all_to_all | solution.py:363
  32.4 14.9 %collective-permute-start.6 = (bf16[8,48,512]{2,1,0:T(8,128)(2,1)}, bf16[8,48,512]{2,1,0:T(8,128)(2,1)}, u32[]{:S(2)}, u32[]{:S(2)}) collective-permute-start(bf16[8,48,512]{2,1,0:T(8,128)(2,1)} %collective-permute-done.rest_2_), channel_id=1, source_target_pairs={{0,6},{1,7},{2,0},{3,1},{4,2},{5,3},{6,4},{7,5},{8,14},{9,15},{10,... | collective-permute-start | bytes 1179656 | tf_op jit(solution)/shard_map/ppermute | solution.py:40
  38.2 9.5 %collective-permute-start.7 = (bf16[4,48,512]{2,1,0:T(8,128)(2,1)}, bf16[4,48,512]{2,1,0:T(8,128)(2,1)}, u32[]{:S(2)}, u32[]{:S(2)}) collective-permute-start(bf16[4,48,512]{2,1,0:T(8,128)(2,1)} %slice.33), channel_id=1, source_target_pairs={{0,6},{1,7},{2,0},{3,1},{4,2},{5,3},{6,4},{7,5},{8,14},{9,15},{10,... | collective-permute-start | bytes 589832 | tf_op jit(solution)/shard_map/ppermute | solution.py:40
  40.2 7.5 %collective-permute-start.8 = (bf16[4,48,512]{2,1,0:T(8,128)(2,1)}, bf16[4,48,512]{2,1,0:T(8,128)(2,1)}, u32[]{:S(2)}, u32[]{:S(2)}) collective-permute-start(bf16[4,48,512]{2,1,0:T(8,128)(2,1)} %slice.34), channel_id=1, source_target_pairs={{0,2},{1,3},{2,4},{3,5},{4,6},{5,7},{6,0},{7,1},{8,10},{9,11},{10,... | collective-permute-start | bytes 589832 | tf_op jit(solution)/shard_map/ppermute | solution.py:37
  47.2 9.9 %copy-start = (bf16[8,48,512]{2,1,0:T(8,128)(2,1)}, bf16[8,48,512]{2,1,0:T(8,128)(2,1)S(1)}, u32[]{:S(2)}) copy-start(bf16[8,48,512]{2,1,0:T(8,128)(2,1)S(1)} %get-tuple-element.77) | copy-start | bytes 1179652
  47.2 9.9 %copy-start.2 = (bf16[8,48,512]{2,1,0:T(8,128)(2,1)}, bf16[8,48,512]{2,1,0:T(8,128)(2,1)S(1)}, u32[]{:S(2)}) copy-start(bf16[8,48,512]{2,1,0:T(8,128)(2,1)S(1)} %get-tuple-element.81) | copy-start | bytes 1179652
  47.3 9.9 %copy-start.11 = (bf16[8,48,512]{2,1,0:T(8,128)(2,1)}, bf16[8,48,512]{2,1,0:T(8,128)(2,1)S(1)}, u32[]{:S(2)}) copy-start(bf16[8,48,512]{2,1,0:T(8,128)(2,1)S(1)} %get-tuple-element.75) | copy-start | bytes 1179652
  57.1 12.7 %collective-permute-start.11 = (f32[2048,128]{1,0:T(8,128)S(1)}, f32[2048,128]{1,0:T(8,128)S(1)}, u32[]{:S(2)}, u32[]{:S(2)}) collective-permute-start(f32[2048,128]{1,0:T(8,128)S(1)} %get-tuple-element.68.after_ref), channel_id=1, source_target_pairs={{0,64},{64,0},{1,65},{65,1},{2,66},{66,2},{3,67},{67,3},{4,68},{68... | collective-permute-start | bytes 3145736 | tf_op jit(solution)/shard_map/ppermute | solution.py:359
  58.7 12.2 %collective-permute-start.9 = (bf16[4,48,512]{2,1,0:T(8,128)(2,1)S(1)}, bf16[4,48,512]{2,1,0:T(8,128)(2,1)S(1)}, u32[]{:S(2)}, u32[]{:S(2)}) collective-permute-start(bf16[4,48,512]{2,1,0:T(8,128)(2,1)S(1)} %get-tuple-element.70), channel_id=1, source_target_pairs={{0,2},{1,3},{2,4},{3,5},{4,6},{5,7},{6,0},{7,1},{8,10},{9,11},{10,... | collective-permute-start | bytes 589832 | tf_op jit(solution)/shard_map/ppermute | solution.py:37
  59.9 11.0 %collective-permute-start.10 = (bf16[4,48,512]{2,1,0:T(8,128)(2,1)S(1)}, bf16[4,48,512]{2,1,0:T(8,128)(2,1)}, u32[]{:S(2)}, u32[]{:S(2)}) collective-permute-start(bf16[4,48,512]{2,1,0:T(8,128)(2,1)S(1)} %get-tuple-element.71), channel_id=1, source_target_pairs={{0,6},{1,7},{2,0},{3,1},{4,2},{5,3},{6,4},{7,5},{8,14},{9,15},{10,... | collective-permute-start | bytes 589832 | tf_op jit(solution)/shard_map/ppermute | solution.py:40
  70.0 22.3 %copy-start.1 = (bf16[8,48,512]{2,1,0:T(8,128)(2,1)S(1)}, bf16[8,48,512]{2,1,0:T(8,128)(2,1)}, u32[]{:S(2)}) copy-start(bf16[8,48,512]{2,1,0:T(8,128)(2,1)} %copy-done) | copy-start | bytes 1179652
  70.9 22.2 %copy-start.21 = (s32[16]{0:T(128)S(1)}, s32[16]{0:T(128)}, u32[]{:S(2)}) copy-start(s32[16]{0:T(128)} %param.8) | copy-start | bytes 196
  70.9 20.5 %all-to-all-start.2 = ((bf16[8,352,128]{2,1,0:T(8,128)(2,1)}), bf16[8,352,128]{2,1,0:T(8,128)(2,1)S(1)}, u32[]{:S(2)}, u32[]{:S(2)}) async-start(bf16[8,352,128]{2,1,0:T(8,128)(2,1)} %pad_maximum_fusion.1), calls=%async_computation.2 | async-start | bytes 1441792 | tf_op jit(solution)/shard_map/all_to_all | solution.py:363
  79.4 21.1 %collective-permute-start.17 = (bf16[8,48,512]{2,1,0:T(8,128)(2,1)}, bf16[8,48,512]{2,1,0:T(8,128)(2,1)}, u32[]{:S(2)}, u32[]{:S(2)}) collective-permute-start(bf16[8,48,512]{2,1,0:T(8,128)(2,1)} %add_convert_fusion.2), channel_id=1, source_target_pairs={{0,6},{1,7},{2,0},{3,1},{4,2},{5,3},{6,4},{7,5},{8,14},{9,15},{10,... | collective-permute-start | bytes 1179656 | tf_op jit(solution)/shard_map/ppermute | solution.py:40
  80.9 22.9 %collective-permute-start.15 = (bf16[8,48,512]{2,1,0:T(8,128)(2,1)}, bf16[8,48,512]{2,1,0:T(8,128)(2,1)}, u32[]{:S(2)}, u32[]{:S(2)}) collective-permute-start(bf16[8,48,512]{2,1,0:T(8,128)(2,1)} %copy-done.12), channel_id=1, source_target_pairs={{0,2},{1,3},{2,4},{3,5},{4,6},{5,7},{6,0},{7,1},{8,10},{9,11},{10,... | collective-permute-start | bytes 1179656 | tf_op jit(solution)/shard_map/ppermute | solution.py:37
  91.4 3.3 %collective-permute-start.12 = (bf16[8,96,128]{2,1,0:T(8,128)(2,1)S(1)}, bf16[8,96,128]{2,1,0:T(8,128)(2,1)S(1)}, u32[]{:S(2)}, u32[]{:S(2)}) collective-permute-start(bf16[8,96,128]{2,1,0:T(8,128)(2,1)S(1)} %slice.35), channel_id=1, source_target_pairs={{0,64},{64,0},{1,65},{65,1},{2,66},{66,2},{3,67},{67,3},{4,68},{68... | collective-permute-start | bytes 589832 | tf_op jit(solution)/shard_map/ppermute | solution.py:359
  93.1 11.0 %collective-permute-start.14 = (bf16[8,48,512]{2,1,0:T(8,128)(2,1)}, bf16[8,48,512]{2,1,0:T(8,128)(2,1)}, u32[]{:S(2)}, u32[]{:S(2)}) collective-permute-start(bf16[8,48,512]{2,1,0:T(8,128)(2,1)} %add_convert_fusion.4), channel_id=1, source_target_pairs={{0,1},{1,0},{2,3},{3,2},{4,5},{5,4},{6,7},{7,6},{8,9},{9,8},{10,11... | collective-permute-start | bytes 1179656 | tf_op jit(solution)/shard_map/ppermute | solution.py:43
  93.2 22.3 %collective-permute-start.13 = (bf16[8,48,512]{2,1,0:T(8,128)(2,1)}, bf16[8,48,512]{2,1,0:T(8,128)(2,1)S(1)}, u32[]{:S(2)}, u32[]{:S(2)}) collective-permute-start(bf16[8,48,512]{2,1,0:T(8,128)(2,1)} %copy-done.11), channel_id=1, source_target_pairs={{0,6},{1,7},{2,0},{3,1},{4,2},{5,3},{6,4},{7,5},{8,14},{9,15},{10,... | collective-permute-start | bytes 1179656 | tf_op jit(solution)/shard_map/ppermute | solution.py:40
  96.3 18.1 %all-to-all-start.3 = ((bf16[8,352,128]{2,1,0:T(8,128)(2,1)}), bf16[8,352,128]{2,1,0:T(8,128)(2,1)}, u32[]{:S(2)}, u32[]{:S(2)}) async-start(bf16[8,352,128]{2,1,0:T(8,128)(2,1)} %assemble.1), calls=%async_computation.3 | async-start | bytes 1441792 | tf_op jit(solution)/shard_map/all_to_all | solution.py:363
  102.3 17.9 %collective-permute-start.18 = (bf16[8,48,512]{2,1,0:T(8,128)(2,1)}, bf16[8,48,512]{2,1,0:T(8,128)(2,1)S(1)}, u32[]{:S(2)}, u32[]{:S(2)}) collective-permute-start(bf16[8,48,512]{2,1,0:T(8,128)(2,1)} %add_convert_fusion.1), channel_id=1, source_target_pairs={{0,1},{1,0},{2,3},{3,2},{4,5},{5,4},{6,7},{7,6},{8,9},{9,8},{10,11... | collective-permute-start | bytes 1179656 | tf_op jit(solution)/shard_map/ppermute | solution.py:43
  106.2 14.0 %collective-permute-start.16 = (bf16[8,48,512]{2,1,0:T(8,128)(2,1)}, bf16[8,48,512]{2,1,0:T(8,128)(2,1)}, u32[]{:S(2)}, u32[]{:S(2)}) collective-permute-start(bf16[8,48,512]{2,1,0:T(8,128)(2,1)} %add_convert_fusion.3), channel_id=1, source_target_pairs={{0,2},{1,3},{2,4},{3,5},{4,6},{5,7},{6,0},{7,1},{8,10},{9,11},{10,... | collective-permute-start | bytes 1179656 | tf_op jit(solution)/shard_map/ppermute | solution.py:37
  114.4 11.1 %collective-permute-start.19 = (bf16[8,352,128]{2,1,0:T(8,128)(2,1)}, bf16[8,352,128]{2,1,0:T(8,128)(2,1)}, u32[]{:S(2)}, u32[]{:S(2)}) collective-permute-start(bf16[8,352,128]{2,1,0:T(8,128)(2,1)} %all-to-all-done.3), channel_id=1, source_target_pairs={{0,64},{64,0},{1,65},{65,1},{2,66},{66,2},{3,67},{67,3},{4,68},{68... | collective-permute-start | bytes 2162696 | tf_op jit(solution)/shard_map/ppermute | solution.py:359
  (14 other events, 58.1 us)
where the time goes:
time: 129 us; the launch traced here: 128 us
  starting transfers between devices  46.4 us (36%)
  waiting for transfers between devices  27.8 us (22%)
  Pallas kernels  25.9 us (20%)
  other arithmetic  15 us (12%)
  local copies, waits for them, and re-layouts  11.4 us (9%)
  between operations  1.65 us (1%)
    all_to_all x4, starting transfers between devices, exchange(): return lax.all_to_all(x, 'dp', 0, 0, tiled=True)  21 us
    all_to_all x4, waiting for transfers between devices, exchange(): return lax.all_to_all(x, 'dp', 0, 0, tiled=True)  20.7 us
    ppermute x6, starting transfers between devices, down(): return lax.ppermute(x, self.name, self.perm_down)  13.9 us
    pallas_call x1, Pallas kernels, kernel_grad(): pl.pallas_call(kernel_grad_kernel, out_shape=[jax.ShapeDtypeStruct((2048,...  9.07 us
    pallas_call x1, Pallas kernels, forward(): pl.pallas_call(forward_kernel, out_shape=[jax.ShapeDtypeStruct((rows, wid...  7.94 us
    convert_element_type x4, other arithmetic, added(): return sum((x.astype(F32) for x in terms)).astype(BF16)  6.51 us
    pallas_call x1, Pallas kernels, input_partials(): pl.pallas_call(input_grad_kernel, out_shape=[whole] * 7 + [half] * 2, in_...  6.09 us
    ppermute x4, starting transfers between devices, core_swap(): return lax.ppermute(x, 'rep', [(0, 1), (1, 0)])  5.98 us
  transfers between devices with their start and end apart: 24, of which 8 were waited for; matrix products, arithmetic and copies ran while one was open for 15% of the time, Pallas kernels for 13%

commit v1 on v0

--- a/solution.py
+++ b/solution.py
@@ -64,7 +64,9 @@
         in_a, in_b = arrived
         got_swap = self.swap(added(pair_next, jnp.concatenate([in_a, jnp.zeros_like(in_a)], 0)))
         got_down = self.down(added(pair_prev, jnp.concatenate([jnp.zeros_like(in_b), in_b], 0)))
-        got_up, from_prev = self.up(second), self.down(prev)
+        got_up = self.up(second)
+        prev, _ = lax.optimization_barrier((prev, got_swap))
+        from_prev = self.down(prev)
         last_up = self.up(added(following, got_swap, got_up))
         last_swap = self.swap(added(pair, got_down))
         return sum(x.astype(F32) for x in (own, from_prev, last_up, last_swap))

time: 129 us -> 130 us (level)
    all_to_all x4, waiting for transfers between devices: 20.7 us -> 16.8 us  [exchange(): return lax.all_to_all(x, 'dp', 0, 0, tiled=True)]
    ppermute x4, waiting for transfers between devices: 5.06 us -> 7.69 us  [swap(): return lax.ppermute(x, self.name, self.perm_swap)]
  transfers between devices with their start and end apart: 24 -> 24, of which waited for: 8 -> 9; matrix products, arithmetic and copies ran while one was open for 15% -> 15% of each run, Pallas kernels for 13% -> 13%
where the time goes in v1:
time: 130 us; the launch traced here: 129 us
  starting transfers between devices  47.6 us (37%)
  waiting for transfers between devices  26.8 us (21%)
  Pallas kernels  25.9 us (20%)
  other arithmetic  15 us (12%)
  local copies, waits for them, and re-layouts  12 us (9%)
  between operations  1.64 us (1%)
    all_to_all x4, starting transfers between devices, exchange(): return lax.all_to_all(x, 'dp', 0, 0, tiled=True)  21.2 us
    all_to_all x4, waiting for transfers between devices, exchange(): return lax.all_to_all(x, 'dp', 0, 0, tiled=True)  16.8 us
    ppermute x6, starting transfers between devices, down(): return lax.ppermute(x, self.name, self.perm_down)  15.1 us
    pallas_call x1, Pallas kernels, kernel_grad(): pl.pallas_call(kernel_grad_kernel, out_shape=[jax.ShapeDtypeStruct((2048,...  9.07 us
    pallas_call x1, Pallas kernels, forward(): pl.pallas_call(forward_kernel, out_shape=[jax.ShapeDtypeStruct((rows, wid...  7.94 us
    ppermute x4, waiting for transfers between devices, swap(): return lax.ppermute(x, self.name, self.perm_swap)  7.69 us
    convert_element_type x4, other arithmetic, added(): return sum((x.astype(F32) for x in terms)).astype(BF16)  6.51 us
    pallas_call x1, Pallas kernels, input_partials(): pl.pallas_call(input_grad_kernel, out_shape=[whole] * 7 + [half] * 2, in_...  6.09 us
  transfers between devices with their start and end apart: 24, of which 9 were waited for; matrix products, arithmetic and copies ran while one was open for 15% of the time, Pallas kernels for 13%

profile of v1, /device:TPU:1, one launch (start us, length us, event | category | flops | bytes accessed | tf_op | source)
XLA Modules:
  0.0 129.0 jit_solution(14271165082919541625)
XLA Ops:
  0.7 1.3 %copy.25 = bf16[8,48,4,128]{3,2,1,0:T(4,128)(2,1)S(1)} copy(bf16[8,48,4,128]{3,0,1,2:T(8,128)(2,1)} %bitcast.49) | data formatting | bytes 786432 | tf_op jit(solution)/shard_map/transpose | solution.py:352
  3.3 4.7 %collective-permute-start = (bf16[8,48,512]{2,1,0:T(8,128)(2,1)S(1)}, bf16[8,48,512]{2,1,0:T(8,128)(2,1)}, u32[]{:S(2)}, u32[]{:S(2)}) collective-permute-start(bf16[8,48,512]{2,1,0:T(8,128)(2,1)S(1)} %reshape.47.rest_0_), channel_id=1, source_target_pairs={{0,6},{1,7},{2,0},{3,1},{4,2},{5,3},{6,4},{7,5},{8,14},{9,15},{10,... | collective-permute-start | bytes 1179656 | tf_op jit(solution)/shard_map/ppermute | solution.py:40
  8.0 1.3 %collective-permute-start.2 = (bf16[8,48,512]{2,1,0:T(8,128)(2,1)S(1)}, bf16[8,48,512]{2,1,0:T(8,128)(2,1)S(1)}, u32[]{:S(2)}, u32[]{:S(2)}) collective-permute-start(bf16[8,48,512]{2,1,0:T(8,128)(2,1)S(1)} %reshape.47.rest_0_), channel_id=1, source_target_pairs={{0,1},{1,0},{2,3},{3,2},{4,5},{5,4},{6,7},{7,6},{8,9},{9,8},{10,11... | collective-permute-start | bytes 1179656 | tf_op jit(solution)/shard_map/ppermute | solution.py:43
  9.3 6.4 %all-to-all-start = ((bf16[8,48,256]{2,1,0:T(8,128)(2,1)}), bf16[8,48,256]{2,1,0:T(8,128)(2,1)S(1)}, u32[]{:S(2)}, u32[]{:S(2)}) async-start(bf16[8,48,256]{2,1,0:T(8,128)(2,1)} %slice.32), calls=%async_computation | async-start | bytes 393216 | tf_op jit(solution)/shard_map/all_to_all | solution.py:365
  19.6 1.3 %collective-permute-start.4 = (bf16[8,48,512]{2,1,0:T(8,128)(2,1)}, bf16[8,48,512]{2,1,0:T(8,128)(2,1)S(1)}, u32[]{:S(2)}, u32[]{:S(2)}) collective-permute-start(bf16[8,48,512]{2,1,0:T(8,128)(2,1)} %collective-permute-done.rest_2_), channel_id=1, source_target_pairs={{0,1},{1,0},{2,3},{3,2},{4,5},{5,4},{6,7},{7,6},{8,9},{9,8},{10,11... | collective-permute-start | bytes 1179656 | tf_op jit(solution)/shard_map/ppermute | solution.py:43
  20.9 2.0 %all-to-all-done.own_ref = bf16[8,48,256]{2,1,0:T(8,128)(2,1)S(1)} async-done(((bf16[8,48,256]{2,1,0:T(8,128)(2,1)}), bf16[8,48,256]{2,1,0:T(8,128)(2,1)S(1)}, u32[]{:S(2)}, u32[]{:S(2)}) %all-to-all-start) | async-done | bytes 196640 | tf_op jit(solution)/shard_map/all_to_all | solution.py:365
  23.0 2.7 %collective-permute-start.3 = (bf16[8,48,256]{2,1,0:T(8,128)(2,1)S(1)}, bf16[8,48,256]{2,1,0:T(8,128)(2,1)S(1)}, u32[]{:S(2)}, u32[]{:S(2)}) collective-permute-start(bf16[8,48,256]{2,1,0:T(8,128)(2,1)S(1)} %all-to-all-done.own_ref), channel_id=1, source_target_pairs={{0,64},{64,0},{1,65},{65,1},{2,66},{66,2},{3,67},{67,3},{4,68},{68... | collective-permute-start | bytes 589832 | tf_op jit(solution)/shard_map/ppermute | solution.py:361
  28.0 3.8 %all-to-all-start.1 = ((bf16[8,48,256]{2,1,0:T(8,128)(2,1)}), bf16[8,48,256]{2,1,0:T(8,128)(2,1)S(1)}, u32[]{:S(2)}, u32[]{:S(2)}) async-start(bf16[8,48,256]{2,1,0:T(8,128)(2,1)} %pick.1), calls=%async_computation.1 | async-start | bytes 393216 | tf_op jit(solution)/shard_map/all_to_all | solution.py:365
  32.4 3.0 %collective-permute-start.6 = (bf16[8,48,512]{2,1,0:T(8,128)(2,1)}, bf16[8,48,512]{2,1,0:T(8,128)(2,1)}, u32[]{:S(2)}, u32[]{:S(2)}) collective-permute-start(bf16[8,48,512]{2,1,0:T(8,128)(2,1)} %collective-permute-done.rest_2_), channel_id=1, source_target_pairs={{0,6},{1,7},{2,0},{3,1},{4,2},{5,3},{6,4},{7,5},{8,14},{9,15},{10,... | collective-permute-start | bytes 1179656 | tf_op jit(solution)/shard_map/ppermute | solution.py:40
  36.0 1.3 %rev.6 = bf16[3,3,3,48,384]{4,3,2,1,0:T(8,128)(2,1)S(1)} reverse(bf16[3,3,3,48,384]{4,3,2,1,0:T(8,128)(2,1)} %bitcast.45), dimensions={1} | reverse | bytes 1990656 | tf_op jit(solution)/shard_map/rev | solution.py:408
  41.1 6.1 %input_partials.1 = (bf16[8,48,512]{2,1,0:T(8,128)(2,1)S(1)}, bf16[8,48,512]{2,1,0:T(8,128)(2,1)S(1)}, bf16[8,48,512]{2,1,0:T(8,128)(2,1)S(1)}, bf16[8,48,512]{2...) custom-call(s32[8]{0:T(128)S(1)} %stack.35.place_ref, ...), custom_call_target="tpu_custom_call" | custom-call | flops 4076863488 | bytes 5000000 | tf_op jit(solution)/shard_map/input_partials/pallas_call | solution.py:269
  48.0 9.1 %kernel_grad.1 = (f32[2048,128]{1,0:T(8,128)S(1)}, f32[2048,128]{1,0:T(8,128)S(1)}) custom-call(s32[8]{0:T(128)S(1)} %stack.35.place_ref, s32[6]{0:T(128)S(1)} %copy-done.15, s32[1]{0:T(128)} %bitcast.11.rep_ref, bf16[8,48,512]{2,1,0:T(8,128)(2,1)S(1)} %get-tuple-element.59.after_ref, bf16[8,48,512]{2,1,0:T(8,128)(2,1)S(1)} %reshape.47.rest_0_, ...), custom_call_target="tpu_custom_call" | custom-call | flops 4076863488 | bytes 6000000 | tf_op jit(solution)/shard_map/kernel_grad/pallas_call | solution.py:331
  57.1 1.6 %collective-permute-start.11 = (f32[2048,128]{1,0:T(8,128)S(1)}, f32[2048,128]{1,0:T(8,128)S(1)}, u32[]{:S(2)}, u32[]{:S(2)}) collective-permute-start(f32[2048,128]{1,0:T(8,128)S(1)} %get-tuple-element.69.after_ref), channel_id=1, source_target_pairs={{0,64},{64,0},{1,65},{65,1},{2,66},{66,2},{3,67},{67,3},{4,68},{68... | collective-permute-start | bytes 3145736 | tf_op jit(solution)/shard_map/ppermute | solution.py:361
  58.7 1.3 %collective-permute-start.9 = (bf16[4,48,512]{2,1,0:T(8,128)(2,1)S(1)}, bf16[4,48,512]{2,1,0:T(8,128)(2,1)S(1)}, u32[]{:S(2)}, u32[]{:S(2)}) collective-permute-start(bf16[4,48,512]{2,1,0:T(8,128)(2,1)S(1)} %get-tuple-element.71), channel_id=1, source_target_pairs={{0,2},{1,3},{2,4},{3,5},{4,6},{5,7},{6,0},{7,1},{8,10},{9,11},{10,... | collective-permute-start | bytes 589832 | tf_op jit(solution)/shard_map/ppermute | solution.py:37
  60.0 2.0 %collective-permute-start.10 = (bf16[4,48,512]{2,1,0:T(8,128)(2,1)S(1)}, bf16[4,48,512]{2,1,0:T(8,128)(2,1)}, u32[]{:S(2)}, u32[]{:S(2)}) collective-permute-start(bf16[4,48,512]{2,1,0:T(8,128)(2,1)S(1)} %get-tuple-element.72), channel_id=1, source_target_pairs={{0,6},{1,7},{2,0},{3,1},{4,2},{5,3},{6,4},{7,5},{8,14},{9,15},{10,... | collective-permute-start | bytes 589832 | tf_op jit(solution)/shard_map/ppermute | solution.py:40
  61.9 7.9 %forward.1 = (f32[8,48,512]{2,1,0:T(8,128)S(1)}, bf16[8,96,128]{2,1,0:T(8,128)(2,1)S(1)}) custom-call(s32[8]{0:T(128)S(1)} %stack.35.place_ref, f32[2048,128]{1,0:T(8,128)S(1)} %get-tuple-element.69.after_ref, bf16[8,48,512]{2,1,0:T(8,128)(2,1)S(1)} %reshape.47.rest_0_, bf16[8,48,512]{2,1,0:T(8,128)(2,1)S(1)} %copy-done.10, ...), custom_call_target="tpu_custom_call" | custom-call | flops 4076863488 | bytes 5000000 | tf_op jit(solution)/shard_map/forward/pallas_call | solution.py:310
  70.9 6.7 %all-to-all-start.2 = ((bf16[8,352,128]{2,1,0:T(8,128)(2,1)}), bf16[8,352,128]{2,1,0:T(8,128)(2,1)S(1)}, u32[]{:S(2)}, u32[]{:S(2)}) async-start(bf16[8,352,128]{2,1,0:T(8,128)(2,1)} %pad_maximum_fusion.1), calls=%async_computation.2 | async-start | bytes 1441792 | tf_op jit(solution)/shard_map/all_to_all | solution.py:365
  77.6 1.8 %add_convert_fusion.2 = bf16[8,48,512]{2,1,0:T(8,128)(2,1)} fusion(bf16[8,48,512]{2,1,0:T(8,128)(2,1)} %copy-done.2, bf16[4,48,512]{2,1,0:T(8,128)(2,1)} %collective-permute-done.10), kind=kLoop, calls=%fused_computation.10 | loop fusion | flops 786432 | bytes 983040 | tf_op jit(solution)/shard_map/convert_element_type | solution.py:76
  79.4 1.5 %collective-permute-start.17 = (bf16[8,48,512]{2,1,0:T(8,128)(2,1)}, bf16[8,48,512]{2,1,0:T(8,128)(2,1)}, u32[]{:S(2)}, u32[]{:S(2)}) collective-permute-start(bf16[8,48,512]{2,1,0:T(8,128)(2,1)} %add_convert_fusion.2), channel_id=1, source_target_pairs={{0,6},{1,7},{2,0},{3,1},{4,2},{5,3},{6,4},{7,5},{8,14},{9,15},{10,... | collective-permute-start | bytes 1179656 | tf_op jit(solution)/shard_map/ppermute | solution.py:40
  80.9 10.5 %all-to-all-done.2.own_ref = bf16[8,352,128]{2,1,0:T(8,128)(2,1)S(1)} async-done(((bf16[8,352,128]{2,1,0:T(8,128)(2,1)}), bf16[8,352,128]{2,1,0:T(8,128)(2,1)S(1)}, u32[]{:S(2)}, u32[]{:S(2)}) %all-to-all-start.2) | async-done | bytes 720928 | tf_op jit(solution)/shard_map/all_to_all | solution.py:365
  93.4 1.5 %assemble.1 = bf16[8,352,128]{2,1,0:T(8,128)(2,1)} custom-call(s32[8]{0:T(128)S(1)} %get-tuple-element.88.row_ref, s32[8]{0:T(128)S(1)} %get-tuple-element.87.from_ref, bf16[8,352,128]{2,1,0:T(8,128)(2,1)S(1)} %all-to-all-done.2.own_ref, bf16[8,96,128]{2,1,0:T(8,128)(2,1)S(1)} %collective-permute-done.12.other_ref), custom_call_target="tpu_custom_call" | custom-call | tf_op jit(solution)/shard_map/assemble/pallas_call | solution.py:297
  94.9 4.3 %all-to-all-start.3 = ((bf16[8,352,128]{2,1,0:T(8,128)(2,1)}), bf16[8,352,128]{2,1,0:T(8,128)(2,1)}, u32[]{:S(2)}, u32[]{:S(2)}) async-start(bf16[8,352,128]{2,1,0:T(8,128)(2,1)} %assemble.1), calls=%async_computation.3 | async-start | bytes 1441792 | tf_op jit(solution)/shard_map/all_to_all | solution.py:365
  99.3 1.8 %add_convert_fusion.1 = bf16[8,48,512]{2,1,0:T(8,128)(2,1)} fusion(bf16[8,48,512]{2,1,0:T(8,128)(2,1)} %collective-permute-done.17, bf16[8,48,512]{2,1,0:T(8,128)(2,1)S(1)} %get-tuple-element.82), kind=kLoop, calls=%fused_computation.9 | loop fusion | flops 786432 | bytes 1179648 | tf_op jit(solution)/shard_map/convert_element_type | solution.py:76
  101.2 1.3 %collective-permute-start.18 = (bf16[8,48,512]{2,1,0:T(8,128)(2,1)}, bf16[8,48,512]{2,1,0:T(8,128)(2,1)S(1)}, u32[]{:S(2)}, u32[]{:S(2)}) collective-permute-start(bf16[8,48,512]{2,1,0:T(8,128)(2,1)} %add_convert_fusion.1), channel_id=1, source_target_pairs={{0,1},{1,0},{2,3},{3,2},{4,5},{5,4},{6,7},{7,6},{8,9},{9,8},{10,11... | collective-permute-start | bytes 1179656 | tf_op jit(solution)/shard_map/ppermute | solution.py:43
  102.4 1.7 %collective-permute-done.13 = bf16[8,48,512]{2,1,0:T(8,128)(2,1)} collective-permute-done((bf16[8,48,512]{2,1,0:T(8,128)(2,1)}, bf16[8,48,512]{2,1,0:T(8,128)(2,1)}, u32[]{:S(2)}, u32[]{:S(2)}) %collective-permute-start.13) | collective-permute-done | bytes 393248 | tf_op jit(solution)/shard_map/ppermute | solution.py:43
  104.2 2.0 %add_convert_fusion.3 = bf16[8,48,512]{2,1,0:T(8,128)(2,1)} fusion(bf16[8,48,512]{2,1,0:T(8,128)(2,1)} %collective-permute-done.15, bf16[8,48,512]{2,1,0:T(8,128)(2,1)} %collective-permute-done.13, bf16[8,48,512]{2,1,0:T(8,128)(2,1)S(1)} %get-tuple-element.80), kind=kLoop, calls=%fused_computation.11 | loop fusion | flops 1179648 | bytes 1572864 | tf_op jit(solution)/shard_map/convert_element_type | solution.py:76
  106.2 2.7 %collective-permute-start.14 = (bf16[8,48,512]{2,1,0:T(8,128)(2,1)S(1)}, bf16[8,48,512]{2,1,0:T(8,128)(2,1)}, u32[]{:S(2)}, u32[]{:S(2)}) collective-permute-start(bf16[8,48,512]{2,1,0:T(8,128)(2,1)S(1)} %copy-done.12), channel_id=1, source_target_pairs={{0,6},{1,7},{2,0},{3,1},{4,2},{5,3},{6,4},{7,5},{8,14},{9,15},{10,... | collective-permute-start | bytes 1179656 | tf_op jit(solution)/shard_map/ppermute | solution.py:40
  108.9 4.3 %all-to-all-done.3 = bf16[8,352,128]{2,1,0:T(8,128)(2,1)} async-done(((bf16[8,352,128]{2,1,0:T(8,128)(2,1)}), bf16[8,352,128]{2,1,0:T(8,128)(2,1)}, u32[]{:S(2)}, u32[]{:S(2)}) %all-to-all-start.3) | async-done | bytes 720928 | tf_op jit(solution)/shard_map/all_to_all | solution.py:365
  114.3 5.9 %collective-permute-done.18 = bf16[8,48,512]{2,1,0:T(8,128)(2,1)S(1)} collective-permute-done((bf16[8,48,512]{2,1,0:T(8,128)(2,1)}, bf16[8,48,512]{2,1,0:T(8,128)(2,1)S(1)}, u32[]{:S(2)}, u32[]{:S(2)}) %collective-permute-start.18) | collective-permute-done | bytes 393248 | tf_op jit(solution)/shard_map/ppermute | solution.py:43
  121.0 1.3 %convert_add_fusion = f32[8,48,512]{2,1,0:T(8,128)S(1)} fusion(bf16[8,48,512]{2,1,0:T(8,128)(2,1)S(1)} %collective-permute-done.18, bf16[8,48,512]{2,1,0:T(8,128)(2,1)} %copy-done.16, bf16[8,48,512]{2,1,0:T(8,128)(2,1)} %collective-permute-done.14, bf16[8,48,512]{2,1,0:T(8,128)(2,1)S(1)} %get-tuple-element.59.after_ref), kind=kLoop, calls=%fused_computation.8 | loop fusion | flops 1376256 | bytes 2359296 | tf_op jit(solution)/shard_map/add | solution.py:72
  122.6 1.3 %copy.36 = f32[8,48,4,128]{3,0,1,2:T(8,128)} copy(f32[8,48,4,128]{3,2,1,0:T(4,128)S(1)} %reshape.51) | data formatting | bytes 1572864 | tf_op jit(solution)/shard_map/reshape | solution.py:357
  127.6 1.4 %copy_bitcast_fusion = f32[48,3,3,3,384]{4,0,3,2,1:T(8,128)} fusion(bf16[3,3,3,3,48,128]{5,4,3,2,1,0:T(8,128)(2,1)S(1)} %bitcast.41), kind=kLoop, calls=%fused_computation | loop fusion | flops 497664 | bytes 2985984 | tf_op jit(solution)/shard_map/convert_element_type | solution.py:438
  (101 shorter events, 21.4 us)
Async XLA Ops:
  0.6 15.0 %copy-start.21 = (s32[16]{0:T(128)S(1)}, s32[16]{0:T(128)}, u32[]{:S(2)}) copy-start(s32[16]{0:T(128)} %param.8) | copy-start | bytes 196
  0.7 16.4 %copy-start.18 = (s32[16]{0:T(128)S(1)}, s32[16]{0:T(128)}, u32[]{:S(2)}) copy-start(s32[16]{0:T(128)} %param.9) | copy-start | bytes 196
  3.3 14.3 %collective-permute-start = (bf16[8,48,512]{2,1,0:T(8,128)(2,1)S(1)}, bf16[8,48,512]{2,1,0:T(8,128)(2,1)}, u32[]{:S(2)}, u32[]{:S(2)}) collective-permute-start(bf16[8,48,512]{2,1,0:T(8,128)(2,1)S(1)} %reshape.47.rest_0_), channel_id=1, source_target_pairs={{0,6},{1,7},{2,0},{3,1},{4,2},{5,3},{6,4},{7,5},{8,14},{9,15},{10,... | collective-permute-start | bytes 1179656 | tf_op jit(solution)/shard_map/ppermute | solution.py:40
  8.0 10.9 %collective-permute-start.1 = (bf16[8,48,512]{2,1,0:T(8,128)(2,1)S(1)}, bf16[8,48,512]{2,1,0:T(8,128)(2,1)S(1)}, u32[]{:S(2)}, u32[]{:S(2)}) collective-permute-start(bf16[8,48,512]{2,1,0:T(8,128)(2,1)S(1)} %reshape.47.rest_0_), channel_id=1, source_target_pairs={{0,2},{1,3},{2,4},{3,5},{4,6},{5,7},{6,0},{7,1},{8,10},{9,11},{10,... | collective-permute-start | bytes 1179656 | tf_op jit(solution)/shard_map/ppermute | solution.py:37
  8.0 11.6 %collective-permute-start.2 = (bf16[8,48,512]{2,1,0:T(8,128)(2,1)S(1)}, bf16[8,48,512]{2,1,0:T(8,128)(2,1)S(1)}, u32[]{:S(2)}, u32[]{:S(2)}) collective-permute-start(bf16[8,48,512]{2,1,0:T(8,128)(2,1)S(1)} %reshape.47.rest_0_), channel_id=1, source_target_pairs={{0,1},{1,0},{2,3},{3,2},{4,5},{5,4},{6,7},{7,6},{8,9},{9,8},{10,11... | collective-permute-start | bytes 1179656 | tf_op jit(solution)/shard_map/ppermute | solution.py:43
  9.3 13.7 %all-to-all-start = ((bf16[8,48,256]{2,1,0:T(8,128)(2,1)}), bf16[8,48,256]{2,1,0:T(8,128)(2,1)S(1)}, u32[]{:S(2)}, u32[]{:S(2)}) async-start(bf16[8,48,256]{2,1,0:T(8,128)(2,1)} %slice.32), calls=%async_computation | async-start | bytes 393216 | tf_op jit(solution)/shard_map/all_to_all | solution.py:365
  19.6 20.8 %copy-start.9 = (bf16[8,48,512]{2,1,0:T(8,128)(2,1)}, bf16[8,48,512]{2,1,0:T(8,128)(2,1)S(1)}, u32[]{:S(2)}) copy-start(bf16[8,48,512]{2,1,0:T(8,128)(2,1)S(1)} %collective-permute-done.2.rest_1_) | copy-start | bytes 1179652
  19.6 17.8 %collective-permute-start.4 = (bf16[8,48,512]{2,1,0:T(8,128)(2,1)}, bf16[8,48,512]{2,1,0:T(8,128)(2,1)S(1)}, u32[]{:S(2)}, u32[]{:S(2)}) collective-permute-start(bf16[8,48,512]{2,1,0:T(8,128)(2,1)} %collective-permute-done.rest_2_), channel_id=1, source_target_pairs={{0,1},{1,0},{2,3},{3,2},{4,5},{5,4},{6,7},{7,6},{8,9},{9,8},{10,11... | collective-permute-start | bytes 1179656 | tf_op jit(solution)/shard_map/ppermute | solution.py:43
  20.9 18.6 %collective-permute-start.5 = (bf16[8,48,512]{2,1,0:T(8,128)(2,1)S(1)}, bf16[8,48,512]{2,1,0:T(8,128)(2,1)S(1)}, u32[]{:S(2)}, u32[]{:S(2)}) collective-permute-start(bf16[8,48,512]{2,1,0:T(8,128)(2,1)S(1)} %collective-permute-done.2.rest_1_), channel_id=1, source_target_pairs={{0,2},{1,3},{2,4},{3,5},{4,6},{5,7},{6,0},{7,1},{8,10},{9,11},{10,... | collective-permute-start | bytes 1179656 | tf_op jit(solution)/shard_map/ppermute | solution.py:37
  23.0 3.7 %collective-permute-start.3 = (bf16[8,48,256]{2,1,0:T(8,128)(2,1)S(1)}, bf16[8,48,256]{2,1,0:T(8,128)(2,1)S(1)}, u32[]{:S(2)}, u32[]{:S(2)}) collective-permute-start(bf16[8,48,256]{2,1,0:T(8,128)(2,1)S(1)} %all-to-all-done.own_ref), channel_id=1, source_target_pairs={{0,64},{64,0},{1,65},{65,1},{2,66},{66,2},{3,67},{67,3},{4,68},{68... | collective-permute-start | bytes 589832 | tf_op jit(solution)/shard_map/ppermute | solution.py:361
  28.0 12.5 %all-to-all-start.1 = ((bf16[8,48,256]{2,1,0:T(8,128)(2,1)}), bf16[8,48,256]{2,1,0:T(8,128)(2,1)S(1)}, u32[]{:S(2)}, u32[]{:S(2)}) async-start(bf16[8,48,256]{2,1,0:T(8,128)(2,1)} %pick.1), calls=%async_computation.1 | async-start | bytes 393216 | tf_op jit(solution)/shard_map/all_to_all | solution.py:365
  32.4 14.8 %collective-permute-start.6 = (bf16[8,48,512]{2,1,0:T(8,128)(2,1)}, bf16[8,48,512]{2,1,0:T(8,128)(2,1)}, u32[]{:S(2)}, u32[]{:S(2)}) collective-permute-start(bf16[8,48,512]{2,1,0:T(8,128)(2,1)} %collective-permute-done.rest_2_), channel_id=1, source_target_pairs={{0,6},{1,7},{2,0},{3,1},{4,2},{5,3},{6,4},{7,5},{8,14},{9,15},{10,... | collective-permute-start | bytes 1179656 | tf_op jit(solution)/shard_map/ppermute | solution.py:40
  38.2 9.6 %collective-permute-start.7 = (bf16[4,48,512]{2,1,0:T(8,128)(2,1)}, bf16[4,48,512]{2,1,0:T(8,128)(2,1)}, u32[]{:S(2)}, u32[]{:S(2)}) collective-permute-start(bf16[4,48,512]{2,1,0:T(8,128)(2,1)} %slice.33), channel_id=1, source_target_pairs={{0,6},{1,7},{2,0},{3,1},{4,2},{5,3},{6,4},{7,5},{8,14},{9,15},{10,... | collective-permute-start | bytes 589832 | tf_op jit(solution)/shard_map/ppermute | solution.py:40
  40.2 7.5 %collective-permute-start.8 = (bf16[4,48,512]{2,1,0:T(8,128)(2,1)}, bf16[4,48,512]{2,1,0:T(8,128)(2,1)}, u32[]{:S(2)}, u32[]{:S(2)}) collective-permute-start(bf16[4,48,512]{2,1,0:T(8,128)(2,1)} %slice.34), channel_id=1, source_target_pairs={{0,2},{1,3},{2,4},{3,5},{4,6},{5,7},{6,0},{7,1},{8,10},{9,11},{10,... | collective-permute-start | bytes 589832 | tf_op jit(solution)/shard_map/ppermute | solution.py:37
  47.2 9.9 %copy-start = (bf16[8,48,512]{2,1,0:T(8,128)(2,1)}, bf16[8,48,512]{2,1,0:T(8,128)(2,1)S(1)}, u32[]{:S(2)}) copy-start(bf16[8,48,512]{2,1,0:T(8,128)(2,1)S(1)} %get-tuple-element.77) | copy-start | bytes 1179652
  47.2 9.9 %copy-start.2 = (bf16[8,48,512]{2,1,0:T(8,128)(2,1)}, bf16[8,48,512]{2,1,0:T(8,128)(2,1)S(1)}, u32[]{:S(2)}) copy-start(bf16[8,48,512]{2,1,0:T(8,128)(2,1)S(1)} %get-tuple-element.83) | copy-start | bytes 1179652
  57.1 12.8 %collective-permute-start.11 = (f32[2048,128]{1,0:T(8,128)S(1)}, f32[2048,128]{1,0:T(8,128)S(1)}, u32[]{:S(2)}, u32[]{:S(2)}) collective-permute-start(f32[2048,128]{1,0:T(8,128)S(1)} %get-tuple-element.69.after_ref), channel_id=1, source_target_pairs={{0,64},{64,0},{1,65},{65,1},{2,66},{66,2},{3,67},{67,3},{4,68},{68... | collective-permute-start | bytes 3145736 | tf_op jit(solution)/shard_map/ppermute | solution.py:361
  58.7 12.3 %collective-permute-start.9 = (bf16[4,48,512]{2,1,0:T(8,128)(2,1)S(1)}, bf16[4,48,512]{2,1,0:T(8,128)(2,1)S(1)}, u32[]{:S(2)}, u32[]{:S(2)}) collective-permute-start(bf16[4,48,512]{2,1,0:T(8,128)(2,1)S(1)} %get-tuple-element.71), channel_id=1, source_target_pairs={{0,2},{1,3},{2,4},{3,5},{4,6},{5,7},{6,0},{7,1},{8,10},{9,11},{10,... | collective-permute-start | bytes 589832 | tf_op jit(solution)/shard_map/ppermute | solution.py:37
  60.0 11.0 %collective-permute-start.10 = (bf16[4,48,512]{2,1,0:T(8,128)(2,1)S(1)}, bf16[4,48,512]{2,1,0:T(8,128)(2,1)}, u32[]{:S(2)}, u32[]{:S(2)}) collective-permute-start(bf16[4,48,512]{2,1,0:T(8,128)(2,1)S(1)} %get-tuple-element.72), channel_id=1, source_target_pairs={{0,6},{1,7},{2,0},{3,1},{4,2},{5,3},{6,4},{7,5},{8,14},{9,15},{10,... | collective-permute-start | bytes 589832 | tf_op jit(solution)/shard_map/ppermute | solution.py:40
  70.0 22.3 %copy-start.1 = (bf16[8,48,512]{2,1,0:T(8,128)(2,1)S(1)}, bf16[8,48,512]{2,1,0:T(8,128)(2,1)}, u32[]{:S(2)}) copy-start(bf16[8,48,512]{2,1,0:T(8,128)(2,1)} %copy-done) | copy-start | bytes 1179652
  70.9 22.2 %copy-start.22 = (s32[16]{0:T(128)S(1)}, s32[16]{0:T(128)}, u32[]{:S(2)}) copy-start(s32[16]{0:T(128)} %param.8) | copy-start | bytes 196
  70.9 20.5 %all-to-all-start.2 = ((bf16[8,352,128]{2,1,0:T(8,128)(2,1)}), bf16[8,352,128]{2,1,0:T(8,128)(2,1)S(1)}, u32[]{:S(2)}, u32[]{:S(2)}) async-start(bf16[8,352,128]{2,1,0:T(8,128)(2,1)} %pad_maximum_fusion.1), calls=%async_computation.2 | async-start | bytes 1441792 | tf_op jit(solution)/shard_map/all_to_all | solution.py:365
  79.4 19.9 %collective-permute-start.17 = (bf16[8,48,512]{2,1,0:T(8,128)(2,1)}, bf16[8,48,512]{2,1,0:T(8,128)(2,1)}, u32[]{:S(2)}, u32[]{:S(2)}) collective-permute-start(bf16[8,48,512]{2,1,0:T(8,128)(2,1)} %add_convert_fusion.2), channel_id=1, source_target_pairs={{0,6},{1,7},{2,0},{3,1},{4,2},{5,3},{6,4},{7,5},{8,14},{9,15},{10,... | collective-permute-start | bytes 1179656 | tf_op jit(solution)/shard_map/ppermute | solution.py:40
  80.9 21.5 %collective-permute-start.15 = (bf16[8,48,512]{2,1,0:T(8,128)(2,1)}, bf16[8,48,512]{2,1,0:T(8,128)(2,1)}, u32[]{:S(2)}, u32[]{:S(2)}) collective-permute-start(bf16[8,48,512]{2,1,0:T(8,128)(2,1)} %copy-done.13), channel_id=1, source_target_pairs={{0,2},{1,3},{2,4},{3,5},{4,6},{5,7},{6,0},{7,1},{8,10},{9,11},{10,... | collective-permute-start | bytes 1179656 | tf_op jit(solution)/shard_map/ppermute | solution.py:37
  91.4 2.0 %collective-permute-start.12 = (bf16[8,96,128]{2,1,0:T(8,128)(2,1)S(1)}, bf16[8,96,128]{2,1,0:T(8,128)(2,1)S(1)}, u32[]{:S(2)}, u32[]{:S(2)}) collective-permute-start(bf16[8,96,128]{2,1,0:T(8,128)(2,1)S(1)} %slice.35), channel_id=1, source_target_pairs={{0,64},{64,0},{1,65},{65,1},{2,66},{66,2},{3,67},{67,3},{4,68},{68... | collective-permute-start | bytes 589832 | tf_op jit(solution)/shard_map/ppermute | solution.py:361
  93.1 11.0 %collective-permute-start.13 = (bf16[8,48,512]{2,1,0:T(8,128)(2,1)}, bf16[8,48,512]{2,1,0:T(8,128)(2,1)}, u32[]{:S(2)}, u32[]{:S(2)}) collective-permute-start(bf16[8,48,512]{2,1,0:T(8,128)(2,1)} %add_convert_fusion.4), channel_id=1, source_target_pairs={{0,1},{1,0},{2,3},{3,2},{4,5},{5,4},{6,7},{7,6},{8,9},{9,8},{10,11... | collective-permute-start | bytes 1179656 | tf_op jit(solution)/shard_map/ppermute | solution.py:43
  94.9 11.3 %copy-start.12 = (bf16[8,48,512]{2,1,0:T(8,128)(2,1)S(1)}, bf16[8,48,512]{2,1,0:T(8,128)(2,1)}, u32[]{:S(2)}) copy-start(bf16[8,48,512]{2,1,0:T(8,128)(2,1)} %copy-done.11) | copy-start | bytes 1179652
  94.9 18.3 %all-to-all-start.3 = ((bf16[8,352,128]{2,1,0:T(8,128)(2,1)}), bf16[8,352,128]{2,1,0:T(8,128)(2,1)}, u32[]{:S(2)}, u32[]{:S(2)}) async-start(bf16[8,352,128]{2,1,0:T(8,128)(2,1)} %assemble.1), calls=%async_computation.3 | async-start | bytes 1441792 | tf_op jit(solution)/shard_map/all_to_all | solution.py:365
  101.2 19.1 %collective-permute-start.18 = (bf16[8,48,512]{2,1,0:T(8,128)(2,1)}, bf16[8,48,512]{2,1,0:T(8,128)(2,1)S(1)}, u32[]{:S(2)}, u32[]{:S(2)}) collective-permute-start(bf16[8,48,512]{2,1,0:T(8,128)(2,1)} %add_convert_fusion.1), channel_id=1, source_target_pairs={{0,1},{1,0},{2,3},{3,2},{4,5},{5,4},{6,7},{7,6},{8,9},{9,8},{10,11... | collective-permute-start | bytes 1179656 | tf_op jit(solution)/shard_map/ppermute | solution.py:43
  106.2 14.0 %collective-permute-start.16 = (bf16[8,48,512]{2,1,0:T(8,128)(2,1)}, bf16[8,48,512]{2,1,0:T(8,128)(2,1)S(1)}, u32[]{:S(2)}, u32[]{:S(2)}) collective-permute-start(bf16[8,48,512]{2,1,0:T(8,128)(2,1)} %add_convert_fusion.3), channel_id=1, source_target_pairs={{0,2},{1,3},{2,4},{3,5},{4,6},{5,7},{6,0},{7,1},{8,10},{9,11},{10,... | collective-permute-start | bytes 1179656 | tf_op jit(solution)/shard_map/ppermute | solution.py:37
  106.2 14.8 %collective-permute-start.14 = (bf16[8,48,512]{2,1,0:T(8,128)(2,1)S(1)}, bf16[8,48,512]{2,1,0:T(8,128)(2,1)}, u32[]{:S(2)}, u32[]{:S(2)}) collective-permute-start(bf16[8,48,512]{2,1,0:T(8,128)(2,1)S(1)} %copy-done.12), channel_id=1, source_target_pairs={{0,6},{1,7},{2,0},{3,1},{4,2},{5,3},{6,4},{7,5},{8,14},{9,15},{10,... | collective-permute-start | bytes 1179656 | tf_op jit(solution)/shard_map/ppermute | solution.py:40
  113.2 13.0 %collective-permute-start.19 = (bf16[8,352,128]{2,1,0:T(8,128)(2,1)}, bf16[8,352,128]{2,1,0:T(8,128)(2,1)}, u32[]{:S(2)}, u32[]{:S(2)}) collective-permute-start(bf16[8,352,128]{2,1,0:T(8,128)(2,1)} %all-to-all-done.3), channel_id=1, source_target_pairs={{0,64},{64,0},{1,65},{65,1},{2,66},{66,2},{3,67},{67,3},{4,68},{68... | collective-permute-start | bytes 2162696 | tf_op jit(solution)/shard_map/ppermute | solution.py:361
  (15 other events, 64.0 us)
